TPU v7x, 256 devices: a whole 4x4x8 slice. The times are simulated.
256 devices in a mesh: va: 8 (over x, y_hi), vb: 8 (over z), occ: 4 (over y_lo, core).
Axes of the slice: x: 4, y: 4 (y_hi: 2, y_lo: 2; y = y_hi * 2 + y_lo), z: 8, core: 2. Of those that a mesh axis runs over, the one named last changes fastest.
Arguments:
- amplitudes: bfloat16 [768, 800, 800], P(('va', 'vb', 'occ')), may hold values from -6 to 6
- integrals: bfloat16 [800, 800, 1024], P('va', ('vb', 'occ')), may hold values from -0.01953125 to 0.01953125
- virt_irrep: int32 [800], replicated, may hold values from 0 to 7
- slab_irrep: int32 [1024], replicated, may hold values from 0 to 7
Outputs:
- ladder: float32 [768, 1024], P(('va', 'vb', 'occ'))
Inputs may be any that keep to these rules, and one draw needn't show every extreme that they name: `virt_irrep`: irrep labels of the D2h group. `slab_irrep`: irrep labels of the D2h group.
All inputs are finite; a program needn't handle non-finite values.
Results may differ from a plain program's by a relative error of at most 0.0003.
Values may be sent and summed in bfloat16 or wider, within the bound.
No kernel may reach another device: no remote copies, remote signals or barrier semaphores. Data moves between devices by JAX's collectives and lax.ppermute only.
A program may use at most 128 MiB of HBM per device.

v0:
```python
import functools

import jax
import jax.numpy as jnp
from jax import lax
from jax.experimental import pallas as pl
from jax.experimental.pallas import tpu as pltpu
from jax.sharding import PartitionSpec as P

LANES = 128
IRREPS = 8
SPARE = 32
CAP = LANES + SPARE
QUARTERS = LANES // SPARE
MIB = 1024 * 1024
SOURCES = ("occ", "va")
AWAYS = (0, 1, 7, 2, 6, 5, 3, 4)


def iota(shape, axis):
    return lax.broadcasted_iota(jnp.int32, shape, axis)


def one_hot(hits):
    return jnp.where(hits, 1.0, 0.0).astype(jnp.bfloat16)


def dot(a, b):
    return jnp.dot(a, b, preferred_element_type=jnp.float32)


def pack_kernel(
    folds, round_ref, second_ref, block_ref, first_ref, row_ref, after_ref,
    low_ref, high_ref, rank_ref, onehot, firsts, masked, part_main, part_over, main, over,
):
    del after_ref
    step = pl.program_id(0)
    per_step, first_width, slab = block_ref.shape
    second_width = per_step * pl.num_programs(0)
    pitch = masked.shape[0] // per_step
    groups = first_width // folds
    square = (LANES, LANES)

    def turned(vector):
        return jnp.transpose(jnp.broadcast_to(vector, square))

    @pl.when(step == 0)
    def _():
        masked[...] = jnp.zeros_like(masked)
        for pad in range(folds * second_width, LANES):
            rows = pl.ds(pad, groups, stride=LANES)
            main[rows, :] = jnp.zeros((groups, LANES), jnp.float32)
            over[rows, :] = jnp.zeros((groups, LANES), jnp.float32)
        firsts[...] = turned(first_ref[...])[: firsts.shape[0]]
        offset = (round_ref[0] * CAP).astype(jnp.float32)
        before = one_hot(iota(square, 0) < iota(square, 1))
        lane = iota((LANES, 2 * LANES), 1).astype(jnp.float32)
        base = jnp.zeros((IRREPS, 1), jnp.float32)
        for k in range(slab // LANES):
            at = slice(k * LANES, (k + 1) * LANES)
            own = iota((IRREPS, LANES), 0).astype(jnp.float32) == row_ref[:, at]
            member = jnp.where(own, 1.0, 0.0)
            count = dot(member.astype(jnp.bfloat16), before) + base
            rank = jnp.sum(jnp.where(own, count, 0.0), axis=0, keepdims=True)
            rank_ref[:, at] = rank.astype(jnp.int32)
            base = base + jnp.sum(member, axis=1, keepdims=True)
            column = turned(rank) - offset
            onehot[at, :] = one_hot(lane == jnp.concatenate([column, column], axis=1))

    for k in range(per_step):
        second = second_ref[step * per_step + k]
        wanted = jnp.bitwise_xor(firsts[...].astype(jnp.int32), second).astype(jnp.float32)
        wanted = wanted[:first_width]
        for t in range(slab // LANES):
            at = slice(t * LANES, (t + 1) * LANES)
            allowed = wanted == row_ref[:, at]
            values = jnp.where(allowed, block_ref[k, :, at].astype(jnp.float32), 0.0)
            masked[k * pitch : k * pitch + first_width, at] = values.astype(jnp.bfloat16)
    packed = dot(masked[...], onehot[...])
    part_main[...] = packed[:, :LANES]
    part_over[...] = packed[:, LANES:]
    for k in range(per_step):
        d = step * per_step + k
        for f in range(folds):
            source = pl.ds(k * pitch + f, groups, stride=folds)
            target = pl.ds(f * second_width + d, groups, stride=LANES)
            main[target, :] = part_main[source, :]
            over[target, :] = part_over[source, :]

    @pl.when(step == pl.num_programs(0) - 1)
    def _():
        per_quarter = groups // QUARTERS
        low = iota(square, 1) < SPARE
        split = groups // 2
        for e in range(per_quarter):
            spare = jnp.zeros(square, jnp.float32)
            for q in range(QUARTERS):
                group = q * per_quarter + e
                rows = slice(group * LANES, (group + 1) * LANES)
                packed = main[rows, :].astype(jnp.bfloat16)
                if group < split:
                    low_ref[group] = packed
                else:
                    high_ref[group - split] = packed
                piece = jnp.where(low, over[rows, :], 0.0)
                spare = spare + (piece if q == 0 else pltpu.roll(piece, q * SPARE, 1))
            spare = spare.astype(jnp.bfloat16)
            if e < per_quarter // 2:
                low_ref[split + e] = spare
            else:
                high_ref[split + e - per_quarter // 2] = spare


def pack_integrals(which, integrals, first_labels, second_labels, slab_irrep, after):
    first_width, second_width, slab = integrals.shape
    folds = LANES // second_width
    groups = first_width // folds
    per_step = 5
    pitch = -(-first_width // 16) * 16
    low = groups // 2 + groups // QUARTERS // 2
    high = groups + groups // QUARTERS - low
    smem = pl.BlockSpec(memory_space=pltpu.SMEM)
    whole = pl.BlockSpec(memory_space=pltpu.VMEM)
    firsts = jnp.pad(first_labels, (0, LANES - first_width)).astype(jnp.float32)
    return pl.pallas_call(
        functools.partial(pack_kernel, folds),
        grid=(second_width // per_step,),
        in_specs=[
            smem,
            smem,
            pl.BlockSpec((per_step, first_width, slab), lambda i: (i, 0, 0)),
            whole,
            whole,
            pl.BlockSpec(memory_space=pl.ANY),
        ],
        out_specs=[whole, whole, whole],
        out_shape=[
            jax.ShapeDtypeStruct((low, LANES, LANES), jnp.bfloat16),
            jax.ShapeDtypeStruct((high, LANES, LANES), jnp.bfloat16),
            jax.ShapeDtypeStruct((1, slab), jnp.int32),
        ],
        scratch_shapes=[
            pltpu.VMEM((slab, 2 * LANES), jnp.bfloat16),
            pltpu.VMEM((pitch, LANES), jnp.float32),
            pltpu.VMEM((per_step * pitch, slab), jnp.bfloat16),
            pltpu.VMEM((per_step * pitch, LANES), jnp.float32),
            pltpu.VMEM((per_step * pitch, LANES), jnp.float32),
            pltpu.VMEM((groups * LANES, LANES), jnp.float32),
            pltpu.VMEM((groups * LANES, LANES), jnp.float32),
        ],
        compiler_params=pltpu.CompilerParams(
            dimension_semantics=("arbitrary",), vmem_limit_bytes=16 * MIB
        ),
        cost_estimate=pl.CostEstimate(
            flops=2 * 2600 * slab * 256, bytes_accessed=6_000_000, transcendentals=0
        ),
        name="pack_integrals",
    )(
        which,
        second_labels,
        jnp.transpose(integrals, (1, 0, 2)),
        firsts.reshape(1, LANES),
        slab_irrep.astype(jnp.float32).reshape(1, slab),
        after,
    )


def spread_kernel(
    folds, second_width, rest, parts, here_ref, amp_ref, out_ref,
    wide, strided, shifted, stage,
):
    virt = amp_ref.shape[1]
    tiles = wide.shape[0]
    tall = virt // folds
    last = (tiles - 1) * LANES
    early = iota((tall, LANES), 1) < LANES // 2
    for t in range(tiles):
        if t < tiles - 1:
            wide[t] = amp_ref[0, :, t * LANES : (t + 1) * LANES].astype(jnp.float32)
        else:
            wide[t] = jnp.zeros((virt, LANES), jnp.float32)
            wide[t, :, : virt - last] = amp_ref[0, :, last:].astype(jnp.float32)
    for f in range(folds):
        held = None
        for t in range(tiles):
            piece = wide[t, pl.ds(f, tall, stride=folds), :]
            strided[f, :, t * LANES : (t + 1) * LANES] = piece.astype(jnp.bfloat16)
            rolled = pltpu.roll(piece, LANES // 2, 1)
            if t > 0:
                shifted[f, :, (t - 1) * LANES : t * LANES] = jnp.where(
                    early, held, rolled
                ).astype(jnp.bfloat16)
            held = rolled
    span = 2 * second_width
    source = iota((LANES, 1), 0)
    lane = iota((LANES, 2 * LANES), 1)
    slots = rest // parts // 2
    for w in range(rest // 2):
        tile, offset = divmod(span * w, LANES)
        held = strided
        if offset + span > LANES:
            held, offset = shifted, offset - LANES // 2
        column = source - offset
        inside = (column >= 0) & (column < span)
        target = column + jnp.where(column >= second_width, LANES - second_width, 0)
        target = jnp.where(inside, target, -LANES)
        at = slice(tile * LANES, (tile + 1) * LANES)
        select = jnp.concatenate(
            [one_hot(lane == target + f * second_width) for f in range(folds)], axis=0
        )
        total = dot(jnp.concatenate([held[f, :, at] for f in range(folds)], axis=1), select)
        for a in range(2):
            outer, inner = divmod(2 * w + a, parts)
            away = lax.rem(outer - here_ref[0] + rest // parts, rest // parts)
            place = sum(jnp.where(away == k, AWAYS.index(k), 0) for k in AWAYS)
            half = place // slots
            stage[half, inner, pl.ds(place - half * slots, tall, stride=slots), :] = total[
                :, a * LANES : (a + 1) * LANES
            ]
    owners = out_ref.shape[1]
    rows = out_ref.shape[3] // 2
    for inner in range(parts):
        for i in range(owners):
            for half in range(2):
                out_ref[inner, i, 0, half * rows : (half + 1) * rows] = stage[
                    half, inner, i * rows : (i + 1) * rows, :
                ].astype(jnp.bfloat16)


def spread_amplitudes(here, amplitudes, owners, outer, parts):
    pairs, virt, _ = amplitudes.shape
    rest = outer * parts
    second_width = virt // rest
    folds = LANES // second_width
    tiles = -(-virt // LANES)
    tall = virt // folds
    rows = tall // owners * outer
    return pl.pallas_call(
        functools.partial(spread_kernel, folds, second_width, rest, parts),
        grid=(pairs,),
        in_specs=[
            pl.BlockSpec(memory_space=pltpu.SMEM),
            pl.BlockSpec((1, virt, virt), lambda p: (p, 0, 0)),
        ],
        out_specs=pl.BlockSpec((parts, owners, 1, rows, LANES), lambda p: (0, 0, p, 0, 0)),
        out_shape=jax.ShapeDtypeStruct((parts, owners, pairs, rows, LANES), jnp.bfloat16),
        scratch_shapes=[
            pltpu.VMEM((tiles, virt, LANES), jnp.float32),
            pltpu.VMEM((folds, tall, tiles * LANES), jnp.bfloat16),
            pltpu.VMEM((folds, tall, (tiles - 1) * LANES), jnp.bfloat16),
            pltpu.VMEM((2, parts, tall * outer // 2, LANES), jnp.float32),
        ],
        compiler_params=pltpu.CompilerParams(
            dimension_semantics=("arbitrary",), vmem_limit_bytes=24 * MIB
        ),
        cost_estimate=pl.CostEstimate(
            flops=2 * 480 * 80 * 65536, bytes_accessed=8_000_000, transcendentals=0
        ),
        name="spread_amplitudes",
    )(here, amplitudes)


def masked_rows(left, at, piece, label):
    tall = piece.shape[0]
    for g in range(IRREPS):
        left[g * tall : (g + 1) * tall, at : at + LANES] = piece * one_hot(label == g)


def contract_kernel(tile, slots, shards, half, amp_ref, labels_ref, *refs):
    refs = list(refs)
    first = half == 0
    start_ref = None if first else refs.pop(0)
    blocks = [(refs[2 * k], refs[2 * k + 1]) for k in range(shards)]
    refs = refs[2 * shards :]
    out_ref = refs.pop(0)
    rest_ref = refs.pop(0) if shards < slots else None
    (amps, labels, turned, left_a, left_b, right, spares, swap,
     amp_sems, block_sems, spare_sems, one_sems) = refs
    all_pairs = amps.shape[1]
    steps = amps.shape[0]
    groups = right.shape[0]
    per_quarter = groups // QUARTERS
    each = tile // slots
    square = tile * tile
    chunk = 2 * all_pairs

    def amp_copy(k):
        at = pl.ds(half * steps * tile + k * tile, tile)
        return pltpu.make_async_copy(amp_ref.at[:, at], amps.at[k], amp_sems.at[k])

    copies = []
    split, cut = groups // 2, per_quarter // 2
    for k, pair in enumerate(blocks):
        for h, block in enumerate(pair):
            copies.append(
                pltpu.make_async_copy(
                    block.at[pl.ds(0, split)],
                    right.at[pl.ds(h * split, split), k, :, pl.ds(0, LANES)],
                    block_sems.at[2 * k + h],
                )
            )
            count = (cut, per_quarter - cut)[h]
            copies.append(
                pltpu.make_async_copy(
                    block.at[pl.ds(split, count)],
                    spares.at[k, pl.ds(h * cut, count)],
                    spare_sems.at[2 * k + h],
                )
            )
    if not first:
        copies.append(pltpu.make_async_copy(start_ref, out_ref, one_sems.at[0]))
    labels_copy = pltpu.make_async_copy(labels_ref, labels, one_sems.at[1])
    amp_copies = [amp_copy(k) for k in range(steps)]
    amp_copies[0].start()
    labels_copy.start()
    for copy in copies:
        copy.start()
    for copy in amp_copies[1:]:
        copy.start()
    order = iota((square, square), 0)
    swap[...] = one_hot(iota((square, square), 1) == (order % tile) * tile + order // tile)
    quarter = iota((1, LANES), 1) // SPARE
    labels_copy.wait()

    def build(k, left):
        amp_copies[k].wait()
        for p in range(0, all_pairs, 2 * tile):
            pieces = [amps[k, q : q + tile].reshape(square, LANES) for q in (p, p + tile)]
            done = dot(swap[...], jnp.concatenate(pieces, axis=1)).astype(jnp.bfloat16)
            for r in range(tile):
                for h in range(2):
                    turned[k % 2, r, p + h * tile : p + (h + 1) * tile, :] = done[
                        r * tile : (r + 1) * tile, h * LANES : (h + 1) * LANES
                    ]
        for r in range(tile):
            group, slot = divmod(r, slots)
            if slot < shards:
                label = labels[k * tile + r : k * tile + r + 1, :]
                masked_rows(left, (group * shards + slot) * LANES, turned[k % 2, r], label)
            else:
                rest_ref[k * each + group] = turned[k % 2, r]

    lefts = (left_a, left_b)
    build(0, left_a)
    for copy in copies:
        copy.wait()
    for c in range(groups):
        keep = one_hot(quarter == c // per_quarter)
        for k in range(shards):
            right[c, k, :, LANES:] = spares[k, c % per_quarter] * keep
    for k in range(steps):
        if k + 1 < steps:
            build(k + 1, lefts[(k + 1) % 2])
        block = right[k * each : (k + 1) * each].reshape(each * shards * LANES, 2 * LANES)
        left = lefts[k % 2]
        for m in range(0, left.shape[0], chunk):
            product = dot(left[m : m + chunk], block)
            if first and k == 0:
                out_ref[m : m + chunk] = product
            else:
                out_ref[m : m + chunk] += product


def contract(amplitudes, labels, start, blocks, half):
    all_pairs, rows, _ = amplitudes.shape
    tile = 16
    slots = 4
    shards = len(blocks)
    groups = rows // (2 * slots)
    per_quarter = groups // QUARTERS
    whole = pl.BlockSpec(memory_space=pltpu.VMEM)
    hbm = pl.BlockSpec(memory_space=pl.ANY)
    steps = rows // 2 // tile
    tall = IRREPS * all_pairs
    wide = tile // slots * shards * LANES
    operands = (() if half == 0 else (start,)) + tuple(sum(blocks, ()))
    out_shape = [jax.ShapeDtypeStruct((tall, 2 * LANES), jnp.float32)]
    if shards < slots:
        out_shape.append(jax.ShapeDtypeStruct((groups, all_pairs, LANES), jnp.bfloat16))
    return pl.pallas_call(
        functools.partial(contract_kernel, tile, slots, shards, half),
        in_specs=[hbm] * (2 + len(operands)),
        out_specs=[whole] * len(out_shape),
        out_shape=out_shape,
        scratch_shapes=[
            pltpu.VMEM((steps, all_pairs, tile, LANES), jnp.bfloat16),
            pltpu.VMEM(labels.shape, labels.dtype),
            pltpu.VMEM((2, tile, all_pairs, LANES), jnp.bfloat16),
            pltpu.VMEM((tall, wide), jnp.bfloat16),
            pltpu.VMEM((tall, wide), jnp.bfloat16),
            pltpu.VMEM((groups, shards, LANES, 2 * LANES), jnp.bfloat16),
            pltpu.VMEM((shards, per_quarter, LANES, LANES), jnp.bfloat16),
            pltpu.VMEM((tile * tile, tile * tile), jnp.bfloat16),
            pltpu.SemaphoreType.DMA((steps,)),
            pltpu.SemaphoreType.DMA((2 * shards,)),
            pltpu.SemaphoreType.DMA((2 * shards,)),
            pltpu.SemaphoreType.DMA((2,)),
        ],
        compiler_params=pltpu.CompilerParams(vmem_limit_bytes=26 * MIB),
        cost_estimate=pl.CostEstimate(
            flops=2 * 768 * 10240 * 256, bytes_accessed=6_000_000, transcendentals=0
        ),
        name="contract",
    )(amplitudes, labels, *operands)


def last_kernel(pairs, slots, cores, core_ref, rest_hbm, labels_hbm, start_hbm, low_hbm, high_hbm,
                mine_ref, other_ref, rest, labels, start, left, right, spares, main, over, sems):
    groups, all_pairs, _ = rest.shape
    per_quarter = groups // QUARTERS
    split, cut = groups // 2, per_quarter // 2
    half = pl.ds(0, LANES)
    first = [
        pltpu.make_async_copy(rest_hbm, rest, sems.at[0]),
        pltpu.make_async_copy(labels_hbm, labels, sems.at[1]),
    ]
    second = [
        pltpu.make_async_copy(
            low_hbm.at[pl.ds(0, split)], right.at[pl.ds(0, split), :, half], sems.at[2]
        ),
        pltpu.make_async_copy(
            high_hbm.at[pl.ds(0, split)], right.at[pl.ds(split, split), :, half], sems.at[3]
        ),
        pltpu.make_async_copy(low_hbm.at[pl.ds(split, cut)], spares.at[pl.ds(0, cut)], sems.at[4]),
        pltpu.make_async_copy(
            high_hbm.at[pl.ds(split, per_quarter - cut)],
            spares.at[pl.ds(cut, per_quarter - cut)],
            sems.at[5],
        ),
    ]
    third = pltpu.make_async_copy(start_hbm, start, sems.at[6])
    for copy in first + second + [third]:
        copy.start()
    for copy in first:
        copy.wait()
    quarter = iota((1, LANES), 1) // SPARE
    for c in range(groups):
        row = c * slots + slots - 1
        masked_rows(left, c * LANES, rest[c], labels[row : row + 1, :])
    for copy in second:
        copy.wait()
    for c in range(groups):
        right[c, :, LANES:] = spares[c % per_quarter] * one_hot(quarter == c // per_quarter)
    product = dot(left[...], right[...].reshape(groups * LANES, 2 * LANES))
    third.wait()
    total = start[...] + product
    main[...] = total[:, :LANES]
    spare = total[:, LANES:]
    spare = spare + pltpu.roll(spare, 2 * SPARE, 1)
    over[...] = spare + pltpu.roll(spare, SPARE, 1)
    owners = all_pairs // pairs
    lines = mine_ref.shape[0] // (owners // cores)
    run = 8
    per = IRREPS // QUARTERS

    def emit(core, ref):
        ref[...] = jnp.zeros_like(ref)
        for block in range(owners // cores // run):
            owner = (block * cores + core) * run
            base = block * run * lines
            for g in range(IRREPS):
                for p in range(pairs):
                    at = g * all_pairs + owner * pairs + p
                    ref[pl.ds(base + g * pairs + p, run, stride=lines), :] = main[
                        pl.ds(at, run, stride=pairs), :
                    ]
            for g in range(per):
                for p in range(pairs):
                    value = jnp.zeros((run, LANES), jnp.float32)
                    for q in range(QUARTERS):
                        at = (q * per + g) * all_pairs + owner * pairs + p
                        piece = over[pl.ds(at, run, stride=pairs), :]
                        value = value + jnp.where(quarter == q, piece, 0.0)
                    at = base + (IRREPS + g) * pairs + p
                    ref[pl.ds(at, run, stride=lines), :] = value

    for core in range(cores):

        @pl.when(core_ref[0] == core)
        def _():
            emit(core, mine_ref)

        @pl.when(core_ref[0] != core)
        def _():
            emit(core, other_ref)


def contract_last(core, rest, labels, start, low, high, pairs):
    groups, all_pairs, _ = rest.shape
    cores = 2
    owners = all_pairs // pairs
    lines = -(-(IRREPS + IRREPS // QUARTERS) * pairs // 8) * 8
    whole = pl.BlockSpec(memory_space=pltpu.VMEM)
    hbm = pl.BlockSpec(memory_space=pl.ANY)
    tall = IRREPS * all_pairs
    shape = jax.ShapeDtypeStruct((owners // cores * lines, LANES), jnp.float32)
    return pl.pallas_call(
        functools.partial(last_kernel, pairs, labels.shape[0] // groups, cores),
        in_specs=[pl.BlockSpec(memory_space=pltpu.SMEM)] + [hbm] * 5,
        out_specs=[whole, whole],
        out_shape=[shape, shape],
        scratch_shapes=[
            pltpu.VMEM(rest.shape, rest.dtype),
            pltpu.VMEM(labels.shape, labels.dtype),
            pltpu.VMEM(start.shape, start.dtype),
            pltpu.VMEM((tall, groups * LANES), jnp.bfloat16),
            pltpu.VMEM((groups, LANES, 2 * LANES), jnp.bfloat16),
            pltpu.VMEM((groups // QUARTERS, LANES, LANES), jnp.bfloat16),
            pltpu.VMEM((tall, LANES), jnp.float32),
            pltpu.VMEM((tall, LANES), jnp.float32),
            pltpu.SemaphoreType.DMA((7,)),
        ],
        compiler_params=pltpu.CompilerParams(vmem_limit_bytes=18 * MIB),
        cost_estimate=pl.CostEstimate(
            flops=2 * 768 * 2560 * 256, bytes_accessed=3_000_000, transcendentals=0
        ),
        name="contract_last",
    )(core, rest, labels, start, low, high)


def unpack_kernel(pairs, round_ref, parts_ref, rank_ref, slab_ref, rest_ref, out_ref):
    rows = parts_ref.shape[1]
    slab = slab_ref.shape[1]
    summed = parts_ref[0]
    for k in range(1, parts_ref.shape[0]):
        summed = summed + parts_ref[k]
    irrep = slab_ref[...]
    rank = rank_ref[...] - round_ref[0] * CAP
    each = IRREPS // QUARTERS
    inside = (rank >= 0) & (rank < CAP)
    spare = rank >= LANES
    target = jnp.where(spare, (irrep // each) * SPARE + rank - LANES, rank)
    target = jnp.where(inside, target, -1)
    pick = jnp.where(iota((LANES, slab), 0) == target, 1.0, 0.0)
    values = jnp.dot(
        summed, pick, preferred_element_type=jnp.float32, precision=lax.Precision.HIGHEST
    )
    first = jnp.where(spare, (IRREPS + irrep % each) * pairs, irrep * pairs)
    row = iota((rows, slab), 0)
    for p in range(pairs):
        out_ref[p : p + 1, :] = rest_ref[p : p + 1, :] + jnp.sum(
            jnp.where(row == first + p, values, 0.0), axis=0, keepdims=True
        )


def unpack(which, parts, rank, slab_irrep, rest):
    pairs, slab = rest.shape
    whole = pl.BlockSpec(memory_space=pltpu.VMEM)
    return pl.pallas_call(
        functools.partial(unpack_kernel, pairs),
        in_specs=[pl.BlockSpec(memory_space=pltpu.SMEM), whole, whole, whole, whole],
        out_specs=whole,
        out_shape=jax.ShapeDtypeStruct((pairs, slab), jnp.float32),
        compiler_params=pltpu.CompilerParams(vmem_limit_bytes=6 * MIB),
        name="unpack",
    )(which, parts, rank, slab_irrep.reshape(1, slab), rest)


def local(amplitudes, integrals, virt_irrep, slab_irrep):
    pairs = amplitudes.shape[0]
    owners = lax.axis_size("va")
    count = lax.axis_size("vb")
    parts = lax.axis_size("occ")
    first_width, second_width, _ = integrals.shape
    folds = LANES // second_width
    groups = first_width // folds
    here = lax.axis_index("vb")
    part = lax.axis_index("occ")

    first_labels = lax.dynamic_slice_in_dim(
        virt_irrep, lax.axis_index("va") * first_width, first_width, 0
    )
    second_labels = lax.dynamic_index_in_dim(
        virt_irrep.reshape(count, parts, second_width), part, 1, keepdims=False
    )
    own_labels = lax.dynamic_index_in_dim(second_labels, here, 0, keepdims=False)
    order = lax.rem(here + jnp.array(AWAYS, jnp.int32), count)
    labels = jnp.bitwise_xor(
        first_labels.reshape(groups, 1, folds, 1),
        jnp.take(second_labels, order, axis=0).reshape(1, count, 1, second_width),
    ).reshape(groups, count, folds * second_width)
    labels = jnp.pad(
        labels, ((0, 0), (0, 0), (0, LANES - folds * second_width)), constant_values=-1
    )
    near_labels = labels[:, : count // 2].reshape(-1, LANES)
    far_labels = labels[:, count // 2 :].reshape(-1, LANES)

    up = [(i, (i + 1) % count) for i in range(count)]
    down = [(i, (i - 1) % count) for i in range(count)]

    same_core = [
        [(2 * k + core) * owners + i for k in range(parts // 2) for i in range(owners)]
        for core in range(2)
    ]

    def shifted(pair, perm):
        return tuple(lax.ppermute(block, "vb", perm) for block in pair)

    def blocks_of(which, after):
        low, high, rank = pack_integrals(
            which, integrals, first_labels, own_labels, slab_irrep, after
        )
        packed = low, high
        r1, l1 = shifted(packed, up), shifted(packed, down)
        r2, l2 = shifted(r1, up), shifted(l1, down)
        r3, l3 = shifted(r2, up), shifted(l2, down)
        return (packed, l1, r1, l2), (r2, r3, l3), rank

    def finish(which, near, middle, rank, arrived, rest_of_sum):
        (start,) = contract(arrived, near_labels, None, near, 0)
        up_end, down_end, start = lax.optimization_barrier((middle[1][0], middle[2][1], start))
        far = lax.ppermute(up_end, "vb", up), lax.ppermute(down_end, "vb", down)
        start, rest = contract(arrived, far_labels, start, middle, 1)
        core = lax.rem(part, 2)
        mine, other = contract_last(core.reshape(1), rest, far_labels, start, *far, pairs)
        partial = mine + lax.ppermute(other, "occ", [(i, i ^ 1) for i in range(parts)])
        partial = partial.reshape(parts // 2 * owners, -1, LANES)
        summands = lax.all_to_all(
            partial, SOURCES, split_axis=0, concat_axis=0, tiled=True, axis_index_groups=same_core
        )
        return unpack(which, summands, rank, slab_irrep, rest_of_sum)

    first = jnp.zeros((1,), jnp.int32)
    spread = spread_amplitudes(here.reshape(1), amplitudes, owners, count, parts)
    sent = spread.reshape((parts * owners,) + spread.shape[2:])
    arrived = lax.all_to_all(sent, SOURCES, split_axis=0, concat_axis=0, tiled=True)
    arrived = arrived.reshape((parts * owners * pairs,) + spread.shape[3:])
    near, middle, rank = blocks_of(first, spread)
    largest = jnp.max(rank)

    def more(carry):
        return carry[0] * CAP <= largest

    def step(carry):
        which = carry[0].reshape(1)
        near, middle, rank = blocks_of(which, spread)
        return carry[0] + 1, finish(which, near, middle, rank, arrived, carry[1])

    nothing = jnp.zeros((pairs, slab_irrep.shape[0]), jnp.float32)
    later = lax.while_loop(more, step, (jnp.int32(1), nothing))[1]
    return finish(first, near, middle, rank, arrived, later)


def solution(mesh):
    return jax.shard_map(
        local,
        mesh=mesh,
        in_specs=(P(("va", "vb", "occ"), None, None), P("va", ("vb", "occ"), None), P(), P()),
        out_specs=P(("va", "vb", "occ"), None),
        check_vma=False,
    )
```

profile of v0, /device:TPU:1, one launch (start us, length us, event | category | flops | bytes accessed | tf_op | source)
XLA Modules:
  0.0 123.0 jit_solution(15707277172032189867)
XLA Ops:
  0.0 2.2 %copy-done = bf16[3,800,800]{2,1,0:T(8,128)(2,1)S(1)} copy-done((bf16[3,800,800]{2,1,0:T(8,128)(2,1)S(1)}, bf16[3,800,800]{2,1,0:T(8,128)(2,1)}, u32[]{:S(2)}) %copy-start) | copy-done | bytes 3840024
  2.2 6.8 %spread_amplitudes.1.after_ref = bf16[4,8,3,160,128]{4,3,2,1,0:T(8,128)(2,1)} custom-call(s32[1]{0:T(128)} %bitcast.7.here_ref, bf16[3,800,800]{2,1,0:T(8,128)(2,1)S(1)} %copy-done), custom_call_target="tpu_custom_call" | custom-call | flops 5033164800 | bytes 8000000 | tf_op jit(solution)/shard_map/spread_amplitudes/pallas_call | solution.py:238
  9.0 8.8 %all-to-all-start.1 = ((bf16[32,3,160,128]{3,2,1,0:T(8,128)(2,1)}), bf16[32,3,160,128]{3,2,1,0:T(8,128)(2,1)}, u32[]{:S(2)}, u32[]{:S(2)}) async-start(bf16[32,3,160,128]{3,2,1,0:T(8,128)(2,1)} %bitcast.34), calls=%async_computation.1 | async-start | bytes 7864320 | tf_op jit(solution)/shard_map/all_to_all | solution.py:626
  17.8 0.0 copy-done.10
  17.8 0.1 reshape.85
  17.9 0.1 dynamic_slice.11
  18.0 0.0 copy-done.9
  18.0 0.0 copy-start.11
  18.0 7.2 %pack_integrals.4 = (bf16[12,128,128]{2,1,0:T(8,128)(2,1)S(1)}, bf16[13,128,128]{2,1,0:T(8,128)(2,1)S(1)}, s32[1,1024]{1,0:T(1,128)S(1)}) custom-call(s32[1]{0:T(128)} %constant.81.clone.1.round_ref, s32[25]{0:T(128)S(1)} %dynamic-slice_bitcast_fusion.second_ref, bf16[25,100,1024]{2,1,0:T(8,128)(2,1)} %bitcast.35, ...), custom_call_target="tpu_custom_call" | custom-call | flops 1363148800 | bytes 6000000 | tf_op jit(solution)/shard_map/pack_integrals/pallas_call | solution.py:125
  25.3 5.7 %collective-permute-start.18 = (bf16[13,128,128]{2,1,0:T(8,128)(2,1)S(1)}, bf16[13,128,128]{2,1,0:T(8,128)(2,1)S(1)}, u32[]{:S(2)}, u32[]{:S(2)}) collective-permute-start(bf16[13,128,128]{2,1,0:T(8,128)(2,1)S(1)} %get-tuple-element.172.refs_1_), channel_id=1, source_target_pairs={{0,28},{4,0},{8,4},{12,8},{16,12},{20,16},{24,20},{28,24},{1,29},{... | collective-permute-start | bytes 1277960 | tf_op jit(solution)/shard_map/ppermute | solution.py:597
  30.9 0.0 collective-permute-start.22
  30.9 2.7 %collective-permute-start.21 = (bf16[12,128,128]{2,1,0:T(8,128)(2,1)S(1)}, bf16[12,128,128]{2,1,0:T(8,128)(2,1)S(1)}, u32[]{:S(2)}, u32[]{:S(2)}) collective-permute-start(bf16[12,128,128]{2,1,0:T(8,128)(2,1)S(1)} %get-tuple-element.171.refs_0_), channel_id=1, source_target_pairs={{0,28},{4,0},{8,4},{12,8},{16,12},{20,16},{24,20},{28,24},{1,29},{... | collective-permute-start | bytes 1179656 | tf_op jit(solution)/shard_map/ppermute | solution.py:597
  33.6 0.0 collective-permute-start.15
  33.6 0.8 copy-done.1
  34.4 0.0 copy-done.11
  34.4 0.6 gather_fusion
  35.0 13.3 %collective-permute-done.21.refs_2_ = bf16[12,128,128]{2,1,0:T(8,128)(2,1)S(1)} collective-permute-done((bf16[12,128,128]{2,1,0:T(8,128)(2,1)S(1)}, bf16[12,128,128]{2,1,0:T(8,128)(2,1)S(1)}, u32[]{:S(2)}, u32[]{:S(2)}) %collective-permute-start.21) | collective-permute-done | bytes 393248 | tf_op jit(solution)/shard_map/ppermute | solution.py:597
  48.3 3.5 %collective-permute-start.23 = (bf16[12,128,128]{2,1,0:T(8,128)(2,1)S(1)}, bf16[12,128,128]{2,1,0:T(8,128)(2,1)}, u32[]{:S(2)}, u32[]{:S(2)}) collective-permute-start(bf16[12,128,128]{2,1,0:T(8,128)(2,1)S(1)} %collective-permute-done.21.refs_2_), channel_id=1, source_target_pairs={{0,28},{4,0},{8,4},{12,8},{16,12},{20,16},{24,20},{28,24},{1,29},{... | collective-permute-start | bytes 1179656 | tf_op jit(solution)/shard_map/ppermute | solution.py:597
  51.8 0.0 collective-permute-done.15.refs_4_
  51.8 0.0 collective-permute-start.16
  51.8 0.8 copy-done.5
  52.5 0.0 collective-permute-done.18.refs_3_
  52.6 2.7 %collective-permute-start.19 = (bf16[13,128,128]{2,1,0:T(8,128)(2,1)S(1)}, bf16[13,128,128]{2,1,0:T(8,128)(2,1)S(1)}, u32[]{:S(2)}, u32[]{:S(2)}) collective-permute-start(bf16[13,128,128]{2,1,0:T(8,128)(2,1)S(1)} %collective-permute-done.18.refs_3_), channel_id=1, source_target_pairs={{0,28},{4,0},{8,4},{12,8},{16,12},{20,16},{24,20},{28,24},{1,29},{... | collective-permute-start | bytes 1277960 | tf_op jit(solution)/shard_map/ppermute | solution.py:597
  55.2 0.0 collective-permute-done.22.refs_5_
  55.2 0.0 collective-permute-start.24
  55.2 0.1 broadcast_select_fusion
  55.3 0.1 xor.24
  55.4 0.1 xor.29
  55.5 0.1 xor.25
  55.6 0.1 xor.26
  55.7 6.7 %collective-permute-done.16.refs_1_ = bf16[12,128,128]{2,1,0:T(8,128)(2,1)} collective-permute-done((bf16[12,128,128]{2,1,0:T(8,128)(2,1)S(1)}, bf16[12,128,128]{2,1,0:T(8,128)(2,1)}, u32[]{:S(2)}, u32[]{:S(2)}) %collective-permute-start.16) | collective-permute-done | bytes 393248 | tf_op jit(solution)/shard_map/ppermute | solution.py:597
  62.4 0.0 collective-permute-start.17
  62.4 5.9 %collective-permute-done.19.refs_7_ = bf16[13,128,128]{2,1,0:T(8,128)(2,1)S(1)} collective-permute-done((bf16[13,128,128]{2,1,0:T(8,128)(2,1)S(1)}, bf16[13,128,128]{2,1,0:T(8,128)(2,1)S(1)}, u32[]{:S(2)}, u32[]{:S(2)}) %collective-permute-start.19) | collective-permute-done | bytes 426016 | tf_op jit(solution)/shard_map/ppermute | solution.py:597
  68.3 3.4 %collective-permute-start.20 = (bf16[13,128,128]{2,1,0:T(8,128)(2,1)S(1)}, bf16[13,128,128]{2,1,0:T(8,128)(2,1)S(1)}, u32[]{:S(2)}, u32[]{:S(2)}) collective-permute-start(bf16[13,128,128]{2,1,0:T(8,128)(2,1)S(1)} %collective-permute-done.19.refs_7_), channel_id=1, source_target_pairs={{0,28},{4,0},{8,4},{12,8},{16,12},{20,16},{24,20},{28,24},{1,29},{... | collective-permute-start | bytes 1277960 | tf_op jit(solution)/shard_map/ppermute | solution.py:597
  71.7 0.0 collective-permute-done.23.refs_6_
  71.7 0.4 collective-permute-start.26
  72.1 0.0 copy-done.3
  72.1 0.0 collective-permute-done.24.refs_2_
  72.1 1.4 %collective-permute-start.25 = (bf16[13,128,128]{2,1,0:T(8,128)(2,1)S(1)}, bf16[13,128,128]{2,1,0:T(8,128)(2,1)S(1)}, u32[]{:S(2)}, u32[]{:S(2)}) collective-permute-start(bf16[13,128,128]{2,1,0:T(8,128)(2,1)S(1)} %collective-permute-done.24.refs_2_), channel_id=1, source_target_pairs={{0,4},{4,8},{8,12},{12,16},{16,20},{20,24},{24,28},{28,0},{1,5},{5... | collective-permute-start | bytes 1277960 | tf_op jit(solution)/shard_map/ppermute | solution.py:597
  73.6 0.0 all-to-all-done.1
  73.6 1.0 copy-done.2
  74.6 1.0 copy-done.4
  75.6 1.0 copy-done.6
  76.6 10.3 %contract.8.refs_0_ = f32[768,256]{1,0:T(8,128)S(1)} custom-call(bf16[96,160,128]{2,1,0:T(8,128)(2,1)} %bitcast.9.amp_ref, s32[80,128]{1,0:T(8,128)S(1)} %bitcast.43, bf16[12,128,128]{2,1,0:T(8,128)(2,1)S(1)} %copy-done.2, bf16[13,128,128]{2,1,0:T(8,128)(2,1)S(1)} %get-tuple-element.172.refs_1_, bf16[12,128,128]{2,1,0:T(8,128)(2,1)S(1)} %copy-done.4, ...), custom_call_target="tpu_custom_call" | custom-call | flops 4026531840 | bytes 6000000 | tf_op jit(solution)/shard_map/contract/pallas_call | solution.py:380
  86.9 0.0 copy-start.7
  86.9 1.0 copy-done.7
  87.9 0.0 collective-permute-done.17.refs_3_
  87.9 0.0 collective-permute-done.20.refs_6_
  87.9 2.0 %collective-permute-start.28 = (bf16[13,128,128]{2,1,0:T(8,128)(2,1)S(1)}, bf16[13,128,128]{2,1,0:T(8,128)(2,1)S(1)}, u32[]{:S(2)}, u32[]{:S(2)}) collective-permute-start(bf16[13,128,128]{2,1,0:T(8,128)(2,1)S(1)} %collective-permute-done.20.refs_6_), channel_id=1, source_target_pairs={{0,28},{4,0},{8,4},{12,8},{16,12},{20,16},{24,20},{28,24},{1,29},{... | collective-permute-start | bytes 1277960 | tf_op jit(solution)/shard_map/ppermute | solution.py:612
  89.9 0.0 collective-permute-start.27
  89.9 0.0 collective-permute-done.26.refs_5_
  89.9 0.0 collective-permute-done.25.refs_4_
  89.9 0.0 copy-start.8
  89.9 1.1 copy-done.8
  91.0 6.9 %contract.9 = (f32[768,256]{1,0:T(8,128)S(1)}, bf16[20,96,128]{2,1,0:T(8,128)(2,1)S(1)}) custom-call(bf16[96,160,128]{2,1,0:T(8,128)(2,1)} %bitcast.9.amp_ref, s32[80,128]{1,0:T(8,128)S(1)} %bitcast.45, f32[768,256]{1,0:T(8,128)S(1)} %copy-done.8, bf16[12,128,128]{2,1,0:T(8,128)(2,1)} %collective-permute-done.16.refs_1_, ...), custom_call_target="tpu_custom_call" | custom-call | flops 4026531840 | bytes 6000000 | tf_op jit(solution)/shard_map/contract/pallas_call | solution.py:380
  97.9 0.9 collective-permute-done.27.low_hbm
  98.8 0.0 collective-permute-done.28.high_hbm
  98.8 3.2 %contract_last.4 = (f32[512,128]{1,0:T(8,128)S(1)}, f32[512,128]{1,0:T(8,128)S(1)}) custom-call(s32[1]{0:T(128)} %bitcast.6.core_ref, bf16[20,96,128]{2,1,0:T(8,128)(2,1)S(1)} %get-tuple-element.174.rest_hbm, s32[80,128]{1,0:T(8,128)S(1)} %bitcast.46, f32[768,256]{1,0:T(8,128)S(1)} %get-tuple-element.175.start_hbm, ...), custom_call_target="tpu_custom_call" | custom-call | flops 1006632960 | bytes 3000000 | tf_op jit(solution)/shard_map/contract_last/pallas_call | solution.py:497
  102.0 4.2 %collective-permute-start.29 = (f32[512,128]{1,0:T(8,128)S(1)}, f32[512,128]{1,0:T(8,128)S(1)}, u32[]{:S(2)}, u32[]{:S(2)}) collective-permute-start(f32[512,128]{1,0:T(8,128)S(1)} %get-tuple-element.179), channel_id=1, source_target_pairs={{0,1},{1,0},{2,3},{3,2},{4,5},{5,4},{6,7},{7,6},{8,9},{9,8},{10,11... | collective-permute-start | bytes 786440 | tf_op jit(solution)/shard_map/ppermute | solution.py:616
  106.1 0.6 reduce_max.9
  106.7 0.6 collective-permute-done.29
  107.3 0.7 while.12
  108.0 13.9 %all_to_all.16.parts_ref = f32[16,32,128]{2,1,0:T(8,128)S(1)} all-to-all(f32[16,32,128]{2,1,0:T(8,128)S(1)} %bitcast.37), channel_id=1, replica_groups={{0,32,64,96,128,160,192,224,2,34,66,98,130,162,194,226},{1,33,65,97,129..., dimensions={0} | all-to-all | bytes 524288 | tf_op jit(solution)/shard_map/all_to_all | solution.py:618
  121.9 1.1 unpack.4
  (20 shorter events, 0.1 us)
Async XLA Ops:
  0.0 2.2 %copy-start = (bf16[3,800,800]{2,1,0:T(8,128)(2,1)S(1)}, bf16[3,800,800]{2,1,0:T(8,128)(2,1)}, u32[]{:S(2)}) copy-start(bf16[3,800,800]{2,1,0:T(8,128)(2,1)} %amp_ref.1) | copy-start | bytes 11520004
  9.0 8.8 %copy-start.10 = (s32[800]{0:T(1024)S(1)}, s32[800]{0:T(1024)}, u32[]{:S(2)}) copy-start(s32[800]{0:T(1024)} %param.9) | copy-start | bytes 9604
  9.0 9.0 %copy-start.9 = (s32[1024]{0:T(1024)S(1)}, s32[1024]{0:T(1024)}, u32[]{:S(2)}) copy-start(s32[1024]{0:T(1024)} %param.10) | copy-start | bytes 12292
  9.0 64.6 %all-to-all-start.1 = ((bf16[32,3,160,128]{3,2,1,0:T(8,128)(2,1)}), bf16[32,3,160,128]{3,2,1,0:T(8,128)(2,1)}, u32[]{:S(2)}, u32[]{:S(2)}) async-start(bf16[32,3,160,128]{3,2,1,0:T(8,128)(2,1)} %bitcast.34), calls=%async_computation.1 | async-start | bytes 7864320 | tf_op jit(solution)/shard_map/all_to_all | solution.py:626
  18.0 16.4 %copy-start.11 = (s32[8]{0:T(128)S(1)}, s32[8]{0:T(128)}, u32[]{:S(2)}) copy-start(s32[8]{0:T(128)} %constant.97.clone) | copy-start | bytes 100
  25.3 27.3 %collective-permute-start.18 = (bf16[13,128,128]{2,1,0:T(8,128)(2,1)S(1)}, bf16[13,128,128]{2,1,0:T(8,128)(2,1)S(1)}, u32[]{:S(2)}, u32[]{:S(2)}) collective-permute-start(bf16[13,128,128]{2,1,0:T(8,128)(2,1)S(1)} %get-tuple-element.172.refs_1_), channel_id=1, source_target_pairs={{0,28},{4,0},{8,4},{12,8},{16,12},{20,16},{24,20},{28,24},{1,29},{... | collective-permute-start | bytes 1277960 | tf_op jit(solution)/shard_map/ppermute | solution.py:597
  30.9 24.3 %collective-permute-start.22 = (bf16[13,128,128]{2,1,0:T(8,128)(2,1)S(1)}, bf16[13,128,128]{2,1,0:T(8,128)(2,1)S(1)}, u32[]{:S(2)}, u32[]{:S(2)}) collective-permute-start(bf16[13,128,128]{2,1,0:T(8,128)(2,1)S(1)} %get-tuple-element.172.refs_1_), channel_id=1, source_target_pairs={{0,4},{4,8},{8,12},{12,16},{16,20},{20,24},{24,28},{28,0},{1,5},{5... | collective-permute-start | bytes 1277960 | tf_op jit(solution)/shard_map/ppermute | solution.py:597
  30.9 17.3 %collective-permute-start.21 = (bf16[12,128,128]{2,1,0:T(8,128)(2,1)S(1)}, bf16[12,128,128]{2,1,0:T(8,128)(2,1)S(1)}, u32[]{:S(2)}, u32[]{:S(2)}) collective-permute-start(bf16[12,128,128]{2,1,0:T(8,128)(2,1)S(1)} %get-tuple-element.171.refs_0_), channel_id=1, source_target_pairs={{0,28},{4,0},{8,4},{12,8},{16,12},{20,16},{24,20},{28,24},{1,29},{... | collective-permute-start | bytes 1179656 | tf_op jit(solution)/shard_map/ppermute | solution.py:597
  33.6 18.2 %collective-permute-start.15 = (bf16[12,128,128]{2,1,0:T(8,128)(2,1)S(1)}, bf16[12,128,128]{2,1,0:T(8,128)(2,1)S(1)}, u32[]{:S(2)}, u32[]{:S(2)}) collective-permute-start(bf16[12,128,128]{2,1,0:T(8,128)(2,1)S(1)} %get-tuple-element.171.refs_0_), channel_id=1, source_target_pairs={{0,4},{4,8},{8,12},{12,16},{16,20},{20,24},{24,28},{28,0},{1,5},{5... | collective-permute-start | bytes 1179656 | tf_op jit(solution)/shard_map/ppermute | solution.py:597
  33.6 0.8 copy-start.1
  48.3 23.9 %copy-start.3 = (bf16[12,128,128]{2,1,0:T(8,128)(2,1)}, bf16[12,128,128]{2,1,0:T(8,128)(2,1)S(1)}, u32[]{:S(2)}) copy-start(bf16[12,128,128]{2,1,0:T(8,128)(2,1)S(1)} %collective-permute-done.21.refs_2_) | copy-start | bytes 1179652
  48.3 23.5 %collective-permute-start.23 = (bf16[12,128,128]{2,1,0:T(8,128)(2,1)S(1)}, bf16[12,128,128]{2,1,0:T(8,128)(2,1)}, u32[]{:S(2)}, u32[]{:S(2)}) collective-permute-start(bf16[12,128,128]{2,1,0:T(8,128)(2,1)S(1)} %collective-permute-done.21.refs_2_), channel_id=1, source_target_pairs={{0,28},{4,0},{8,4},{12,8},{16,12},{20,16},{24,20},{28,24},{1,29},{... | collective-permute-start | bytes 1179656 | tf_op jit(solution)/shard_map/ppermute | solution.py:597
  51.8 10.6 %collective-permute-start.16 = (bf16[12,128,128]{2,1,0:T(8,128)(2,1)S(1)}, bf16[12,128,128]{2,1,0:T(8,128)(2,1)}, u32[]{:S(2)}, u32[]{:S(2)}) collective-permute-start(bf16[12,128,128]{2,1,0:T(8,128)(2,1)S(1)} %collective-permute-done.15.refs_4_), channel_id=1, source_target_pairs={{0,4},{4,8},{8,12},{12,16},{16,20},{20,24},{24,28},{28,0},{1,5},{5... | collective-permute-start | bytes 1179656 | tf_op jit(solution)/shard_map/ppermute | solution.py:597
  51.8 0.8 copy-start.5
  52.6 15.8 %collective-permute-start.19 = (bf16[13,128,128]{2,1,0:T(8,128)(2,1)S(1)}, bf16[13,128,128]{2,1,0:T(8,128)(2,1)S(1)}, u32[]{:S(2)}, u32[]{:S(2)}) collective-permute-start(bf16[13,128,128]{2,1,0:T(8,128)(2,1)S(1)} %collective-permute-done.18.refs_3_), channel_id=1, source_target_pairs={{0,28},{4,0},{8,4},{12,8},{16,12},{20,16},{24,20},{28,24},{1,29},{... | collective-permute-start | bytes 1277960 | tf_op jit(solution)/shard_map/ppermute | solution.py:597
  55.2 16.9 %collective-permute-start.24 = (bf16[13,128,128]{2,1,0:T(8,128)(2,1)S(1)}, bf16[13,128,128]{2,1,0:T(8,128)(2,1)S(1)}, u32[]{:S(2)}, u32[]{:S(2)}) collective-permute-start(bf16[13,128,128]{2,1,0:T(8,128)(2,1)S(1)} %collective-permute-done.22.refs_5_), channel_id=1, source_target_pairs={{0,4},{4,8},{8,12},{12,16},{16,20},{20,24},{24,28},{28,0},{1,5},{5... | collective-permute-start | bytes 1277960 | tf_op jit(solution)/shard_map/ppermute | solution.py:597
  62.4 25.5 %collective-permute-start.17 = (bf16[12,128,128]{2,1,0:T(8,128)(2,1)}, bf16[12,128,128]{2,1,0:T(8,128)(2,1)}, u32[]{:S(2)}, u32[]{:S(2)}) collective-permute-start(bf16[12,128,128]{2,1,0:T(8,128)(2,1)} %collective-permute-done.16.refs_1_), channel_id=1, source_target_pairs={{0,4},{4,8},{8,12},{12,16},{16,20},{20,24},{24,28},{28,0},{1,5},{5... | collective-permute-start | bytes 1179656 | tf_op jit(solution)/shard_map/ppermute | solution.py:597
  68.3 19.6 %collective-permute-start.20 = (bf16[13,128,128]{2,1,0:T(8,128)(2,1)S(1)}, bf16[13,128,128]{2,1,0:T(8,128)(2,1)S(1)}, u32[]{:S(2)}, u32[]{:S(2)}) collective-permute-start(bf16[13,128,128]{2,1,0:T(8,128)(2,1)S(1)} %collective-permute-done.19.refs_7_), channel_id=1, source_target_pairs={{0,28},{4,0},{8,4},{12,8},{16,12},{20,16},{24,20},{28,24},{1,29},{... | collective-permute-start | bytes 1277960 | tf_op jit(solution)/shard_map/ppermute | solution.py:597
  71.7 18.1 %collective-permute-start.26 = (bf16[12,128,128]{2,1,0:T(8,128)(2,1)}, bf16[12,128,128]{2,1,0:T(8,128)(2,1)}, u32[]{:S(2)}, u32[]{:S(2)}) collective-permute-start(bf16[12,128,128]{2,1,0:T(8,128)(2,1)} %collective-permute-done.23.refs_6_), channel_id=1, source_target_pairs={{0,28},{4,0},{8,4},{12,8},{16,12},{20,16},{24,20},{28,24},{1,29},{... | collective-permute-start | bytes 1179656 | tf_op jit(solution)/shard_map/ppermute | solution.py:597
  72.1 17.7 %collective-permute-start.25 = (bf16[13,128,128]{2,1,0:T(8,128)(2,1)S(1)}, bf16[13,128,128]{2,1,0:T(8,128)(2,1)S(1)}, u32[]{:S(2)}, u32[]{:S(2)}) collective-permute-start(bf16[13,128,128]{2,1,0:T(8,128)(2,1)S(1)} %collective-permute-done.24.refs_2_), channel_id=1, source_target_pairs={{0,4},{4,8},{8,12},{12,16},{16,20},{20,24},{24,28},{28,0},{1,5},{5... | collective-permute-start | bytes 1277960 | tf_op jit(solution)/shard_map/ppermute | solution.py:597
  73.6 1.0 copy-start.2
  74.6 1.0 copy-start.4
  75.6 1.0 copy-start.6
  86.9 1.0 copy-start.7
  87.9 10.9 %collective-permute-start.28 = (bf16[13,128,128]{2,1,0:T(8,128)(2,1)S(1)}, bf16[13,128,128]{2,1,0:T(8,128)(2,1)S(1)}, u32[]{:S(2)}, u32[]{:S(2)}) collective-permute-start(bf16[13,128,128]{2,1,0:T(8,128)(2,1)S(1)} %collective-permute-done.20.refs_6_), channel_id=1, source_target_pairs={{0,28},{4,0},{8,4},{12,8},{16,12},{20,16},{24,20},{28,24},{1,29},{... | collective-permute-start | bytes 1277960 | tf_op jit(solution)/shard_map/ppermute | solution.py:612
  89.9 8.9 %collective-permute-start.27 = (bf16[12,128,128]{2,1,0:T(8,128)(2,1)}, bf16[12,128,128]{2,1,0:T(8,128)(2,1)S(1)}, u32[]{:S(2)}, u32[]{:S(2)}) collective-permute-start(bf16[12,128,128]{2,1,0:T(8,128)(2,1)} %collective-permute-done.17.refs_3_), channel_id=1, source_target_pairs={{0,4},{4,8},{8,12},{12,16},{16,20},{20,24},{24,28},{28,0},{1,5},{5... | collective-permute-start | bytes 1179656 | tf_op jit(solution)/shard_map/ppermute | solution.py:612
  89.9 1.1 copy-start.8
  102.0 5.3 %collective-permute-start.29 = (f32[512,128]{1,0:T(8,128)S(1)}, f32[512,128]{1,0:T(8,128)S(1)}, u32[]{:S(2)}, u32[]{:S(2)}) collective-permute-start(f32[512,128]{1,0:T(8,128)S(1)} %get-tuple-element.179), channel_id=1, source_target_pairs={{0,1},{1,0},{2,3},{3,2},{4,5},{5,4},{6,7},{7,6},{8,9},{9,8},{10,11... | collective-permute-start | bytes 786440 | tf_op jit(solution)/shard_map/ppermute | solution.py:616
where the time goes:
time: 124 us; the launch traced here: 123 us
  Pallas kernels  35.5 us (29%)
  starting transfers between devices  34.7 us (28%)
  waiting for transfers between devices  27.3 us (22%)
  blocking collectives  13.9 us (11%)
  local copies, waits for them, and re-layouts  9.95 us (8%)
    ppermute x12, waiting for transfers between devices, shifted(): return tuple((lax.ppermute(block, 'vb', perm) for block in pair))  25.9 us
    ppermute x12, starting transfers between devices, shifted(): return tuple((lax.ppermute(block, 'vb', perm) for block in pair))  19.7 us
    pallas_call x2, Pallas kernels, contract(): pl.pallas_call(functools.partial(contract_kernel, tile, slots, shards, ha...  17.2 us
    all_to_all x1, blocking collectives, finish(): lax.all_to_all(partial, SOURCES, split_axis=0, concat_axis=0, tiled=True,...  13.9 us
    unnamed x24, local copies, waits for them, and re-layouts  8.85 us
    all_to_all x1, starting transfers between devices, local(): lax.all_to_all(sent, SOURCES, split_axis=0, concat_axis=0, tiled=True)  8.77 us
    pallas_call x1, Pallas kernels, pack_integrals(): pl.pallas_call(functools.partial(pack_kernel, folds), grid=(second_width...  7.23 us
    pallas_call x1, Pallas kernels, spread_amplitudes(): pl.pallas_call(functools.partial(spread_kernel, folds, second_width, rest...  6.78 us
  transfers between devices with their start and end apart: 16, of which 5 were waited for; matrix products, arithmetic and copies ran while one was open for 1% of the time, Pallas kernels for 20%

commit v1 on v0

--- a/solution.py
+++ b/solution.py
@@ -251,7 +251,7 @@
             pltpu.VMEM((2, parts, tall * outer // 2, LANES), jnp.float32),
         ],
         compiler_params=pltpu.CompilerParams(
-            dimension_semantics=("arbitrary",), vmem_limit_bytes=24 * MIB
+            dimension_semantics=("arbitrary",), vmem_limit_bytes=56 * MIB
         ),
         cost_estimate=pl.CostEstimate(
             flops=2 * 480 * 80 * 65536, bytes_accessed=8_000_000, transcendentals=0
@@ -396,7 +396,7 @@
             pltpu.SemaphoreType.DMA((2 * shards,)),
             pltpu.SemaphoreType.DMA((2,)),
         ],
-        compiler_params=pltpu.CompilerParams(vmem_limit_bytes=26 * MIB),
+        compiler_params=pltpu.CompilerParams(vmem_limit_bytes=(26 if half else 56) * MIB),
         cost_estimate=pl.CostEstimate(
             flops=2 * 768 * 10240 * 256, bytes_accessed=6_000_000, transcendentals=0
         ),
@@ -610,6 +610,7 @@
         (start,) = contract(arrived, near_labels, None, near, 0)
         up_end, down_end, start = lax.optimization_barrier((middle[1][0], middle[2][1], start))
         far = lax.ppermute(up_end, "vb", up), lax.ppermute(down_end, "vb", down)
+        start, rest_of_sum = lax.optimization_barrier((start, rest_of_sum))
         start, rest = contract(arrived, far_labels, start, middle, 1)
         core = lax.rem(part, 2)
         mine, other = contract_last(core.reshape(1), rest, far_labels, start, *far, pairs)

time: 124 us -> 159 us (1.28)
  waiting for transfers between devices: 27.3 us -> 74 us
  local copies, waits for them, and re-layouts: 9.95 us -> 2.28 us
  blocking collectives: 13.9 us -> 10.6 us
  starting transfers between devices: 34.7 us -> 32 us
  Pallas kernels: 35.5 us -> 37.9 us
    all_to_all x1, waiting for transfers between devices: 0.01 us -> 37.3 us  [local(): lax.all_to_all(sent, SOURCES, split_axis=0, concat_axis=0, tiled=True)]
    ppermute x12, waiting for transfers between devices: 25.9 us -> 35.5 us  [shifted(): return tuple((lax.ppermute(block, 'vb', perm) for block in pair))]
    unnamed x24, local copies, waits for them, and re-layouts: 8.85 us -> 1.18 us
    all_to_all x1, blocking collectives: 13.9 us -> 10.6 us  [finish(): lax.all_to_all(partial, SOURCES, split_axis=0, concat_axis=0, tiled=True,...]
    ppermute x1, starting transfers between devices: 4.16 us -> 2.15 us  [finish(): lax.ppermute(other, 'occ', [(i, i ^ 1) for i in range(parts)])]
  transfers between devices with their start and end apart: 16 -> 16, of which waited for: 5 -> 6; matrix products, arithmetic and copies ran while one was open for 1% -> 1% of each run, Pallas kernels for 20% -> 16%
where the time goes in v1:
time: 159 us
  waiting for transfers between devices  74 us (47%)
  Pallas kernels  37.9 us (24%)
  starting transfers between devices  32 us (20%)
  blocking collectives  10.6 us (7%)
  local copies, waits for them, and re-layouts  2.28 us (1%)
    all_to_all x1, waiting for transfers between devices, local(): lax.all_to_all(sent, SOURCES, split_axis=0, concat_axis=0, tiled=True)  37.3 us
    ppermute x12, waiting for transfers between devices, shifted(): return tuple((lax.ppermute(block, 'vb', perm) for block in pair))  35.5 us
    pallas_call x2, Pallas kernels, contract(): pl.pallas_call(functools.partial(contract_kernel, tile, slots, shards, ha...  18.3 us
    ppermute x12, starting transfers between devices, shifted(): return tuple((lax.ppermute(block, 'vb', perm) for block in pair))  18.3 us
    all_to_all x1, blocking collectives, finish(): lax.all_to_all(partial, SOURCES, split_axis=0, concat_axis=0, tiled=True,...  10.6 us
    all_to_all x1, starting transfers between devices, local(): lax.all_to_all(sent, SOURCES, split_axis=0, concat_axis=0, tiled=True)  8.76 us
    pallas_call x1, Pallas kernels, spread_amplitudes(): pl.pallas_call(functools.partial(spread_kernel, folds, second_width, rest...  8.08 us
    pallas_call x1, Pallas kernels, pack_integrals(): pl.pallas_call(functools.partial(pack_kernel, folds), grid=(second_width...  7.23 us
  transfers between devices with their start and end apart: 16, of which 6 were waited for; matrix products, arithmetic and copies ran while one was open for 1% of the time, Pallas kernels for 16%

profile of v1, /device:TPU:1, one launch (start us, length us, event | category | flops | bytes accessed | tf_op | source)
XLA Modules:
  0.0 158.7 jit_solution(978257782445327261)
XLA Ops:
  0.0 8.1 %spread_amplitudes.1.after_ref = bf16[4,8,3,160,128]{4,3,2,1,0:T(8,128)(2,1)} custom-call(s32[1]{0:T(128)} %bitcast.7.here_ref, bf16[3,800,800]{2,1,0:T(8,128)(2,1)} %amp_ref.1), custom_call_target="tpu_custom_call" | custom-call | flops 5033164800 | bytes 8000000 | tf_op jit(solution)/shard_map/spread_amplitudes/pallas_call | solution.py:238
  8.1 8.8 %all-to-all-start.1 = ((bf16[32,3,160,128]{3,2,1,0:T(8,128)(2,1)}), bf16[32,3,160,128]{3,2,1,0:T(8,128)(2,1)}, u32[]{:S(2)}, u32[]{:S(2)}) async-start(bf16[32,3,160,128]{3,2,1,0:T(8,128)(2,1)} %bitcast.34), calls=%async_computation.1 | async-start | bytes 7864320 | tf_op jit(solution)/shard_map/all_to_all | solution.py:627
  16.9 0.0 copy-done.7
  16.9 0.1 reshape.85
  17.0 0.1 dynamic_slice.11
  17.1 0.0 copy-done.6
  17.1 0.0 copy-start.8
  17.1 7.2 %pack_integrals.4 = (bf16[12,128,128]{2,1,0:T(8,128)(2,1)S(1)}, bf16[13,128,128]{2,1,0:T(8,128)(2,1)S(1)}, s32[1,1024]{1,0:T(1,128)S(1)}) custom-call(s32[1]{0:T(128)} %constant.81.clone.1.round_ref, s32[25]{0:T(128)S(1)} %dynamic-slice_bitcast_fusion.second_ref, bf16[25,100,1024]{2,1,0:T(8,128)(2,1)} %bitcast.35, ...), custom_call_target="tpu_custom_call" | custom-call | flops 1363148800 | bytes 6000000 | tf_op jit(solution)/shard_map/pack_integrals/pallas_call | solution.py:125
  24.3 0.0 copy-start
  24.4 0.0 copy-start.2
  24.4 5.7 %collective-permute-start.18 = (bf16[13,128,128]{2,1,0:T(8,128)(2,1)S(1)}, bf16[13,128,128]{2,1,0:T(8,128)(2,1)S(1)}, u32[]{:S(2)}, u32[]{:S(2)}) collective-permute-start(bf16[13,128,128]{2,1,0:T(8,128)(2,1)S(1)} %get-tuple-element.177.refs_1_), channel_id=1, source_target_pairs={{0,28},{4,0},{8,4},{12,8},{16,12},{20,16},{24,20},{28,24},{1,29},{... | collective-permute-start | bytes 1277960 | tf_op jit(solution)/shard_map/ppermute | solution.py:597
  30.0 0.1 xor.24
  30.1 0.0 copy-done.8
  30.2 0.6 gather_fusion
  30.7 0.1 broadcast_select_fusion
  30.8 0.1 xor.29
  30.9 0.1 xor.25
  31.0 0.1 xor.26
  31.1 0.7 reduce_max.9
  31.8 37.3 %all-to-all-done.1 = bf16[32,3,160,128]{3,2,1,0:T(8,128)(2,1)} async-done(((bf16[32,3,160,128]{3,2,1,0:T(8,128)(2,1)}), bf16[32,3,160,128]{3,2,1,0:T(8,128)(2,1)}, u32[]{:S(2)}, u32[]{:S(2)}) %all-to-all-start.1) | async-done | bytes 3932192 | tf_op jit(solution)/shard_map/all_to_all | solution.py:627
  69.1 0.8 while.12
  69.9 0.0 copy-done
  69.9 1.7 %collective-permute-start.22 = (bf16[13,128,128]{2,1,0:T(8,128)(2,1)S(1)}, bf16[13,128,128]{2,1,0:T(8,128)(2,1)S(1)}, u32[]{:S(2)}, u32[]{:S(2)}) collective-permute-start(bf16[13,128,128]{2,1,0:T(8,128)(2,1)S(1)} %get-tuple-element.177.refs_1_), channel_id=1, source_target_pairs={{0,4},{4,8},{8,12},{12,16},{16,20},{20,24},{24,28},{28,0},{1,5},{5... | collective-permute-start | bytes 1277960 | tf_op jit(solution)/shard_map/ppermute | solution.py:597
  71.6 1.6 %collective-permute-start.15 = (bf16[12,128,128]{2,1,0:T(8,128)(2,1)S(1)}, bf16[12,128,128]{2,1,0:T(8,128)(2,1)S(1)}, u32[]{:S(2)}, u32[]{:S(2)}) collective-permute-start(bf16[12,128,128]{2,1,0:T(8,128)(2,1)S(1)} %get-tuple-element.176.refs_0_), channel_id=1, source_target_pairs={{0,4},{4,8},{8,12},{12,16},{16,20},{20,24},{24,28},{28,0},{1,5},{5... | collective-permute-start | bytes 1179656 | tf_op jit(solution)/shard_map/ppermute | solution.py:597
  73.2 0.0 copy-done.2
  73.2 2.5 %collective-permute-start.21 = (bf16[12,128,128]{2,1,0:T(8,128)(2,1)S(1)}, bf16[12,128,128]{2,1,0:T(8,128)(2,1)S(1)}, u32[]{:S(2)}, u32[]{:S(2)}) collective-permute-start(bf16[12,128,128]{2,1,0:T(8,128)(2,1)S(1)} %get-tuple-element.176.refs_0_), channel_id=1, source_target_pairs={{0,28},{4,0},{8,4},{12,8},{16,12},{20,16},{24,20},{28,24},{1,29},{... | collective-permute-start | bytes 1179656 | tf_op jit(solution)/shard_map/ppermute | solution.py:597
  75.7 0.0 collective-permute-done.18.refs_3_
  75.7 1.4 collective-permute-start.19
  77.1 8.7 %collective-permute-done.22.refs_5_ = bf16[13,128,128]{2,1,0:T(8,128)(2,1)S(1)} collective-permute-done((bf16[13,128,128]{2,1,0:T(8,128)(2,1)S(1)}, bf16[13,128,128]{2,1,0:T(8,128)(2,1)S(1)}, u32[]{:S(2)}, u32[]{:S(2)}) %collective-permute-start.22) | collective-permute-done | bytes 426016 | tf_op jit(solution)/shard_map/ppermute | solution.py:597
  85.8 0.0 collective-permute-start.24
  85.8 8.4 %collective-permute-done.15.refs_4_ = bf16[12,128,128]{2,1,0:T(8,128)(2,1)S(1)} collective-permute-done((bf16[12,128,128]{2,1,0:T(8,128)(2,1)S(1)}, bf16[12,128,128]{2,1,0:T(8,128)(2,1)S(1)}, u32[]{:S(2)}, u32[]{:S(2)}) %collective-permute-start.15) | collective-permute-done | bytes 393248 | tf_op jit(solution)/shard_map/ppermute | solution.py:597
  94.2 0.0 collective-permute-start.16
  94.2 0.0 collective-permute-done.21.refs_2_
  94.2 0.0 copy-start.17
  94.2 2.7 %collective-permute-start.23 = (bf16[12,128,128]{2,1,0:T(8,128)(2,1)S(1)}, bf16[12,128,128]{2,1,0:T(8,128)(2,1)S(1)}, u32[]{:S(2)}, u32[]{:S(2)}) collective-permute-start(bf16[12,128,128]{2,1,0:T(8,128)(2,1)S(1)} %collective-permute-done.21.refs_2_), channel_id=1, source_target_pairs={{0,28},{4,0},{8,4},{12,8},{16,12},{20,16},{24,20},{28,24},{1,29},{... | collective-permute-start | bytes 1179656 | tf_op jit(solution)/shard_map/ppermute | solution.py:597
  96.9 0.0 collective-permute-done.19.refs_7_
  96.9 0.1 collective-permute-start.20
  97.0 14.8 %collective-permute-done.16.refs_1_ = bf16[12,128,128]{2,1,0:T(8,128)(2,1)S(1)} collective-permute-done((bf16[12,128,128]{2,1,0:T(8,128)(2,1)S(1)}, bf16[12,128,128]{2,1,0:T(8,128)(2,1)S(1)}, u32[]{:S(2)}, u32[]{:S(2)}) %collective-permute-start.16) | collective-permute-done | bytes 393248 | tf_op jit(solution)/shard_map/ppermute | solution.py:597
  111.7 0.0 collective-permute-start.17
  111.7 0.0 collective-permute-done.23.refs_6_
  111.7 2.7 %collective-permute-start.26 = (bf16[12,128,128]{2,1,0:T(8,128)(2,1)S(1)}, bf16[12,128,128]{2,1,0:T(8,128)(2,1)S(1)}, u32[]{:S(2)}, u32[]{:S(2)}) collective-permute-start(bf16[12,128,128]{2,1,0:T(8,128)(2,1)S(1)} %collective-permute-done.23.refs_6_), channel_id=1, source_target_pairs={{0,28},{4,0},{8,4},{12,8},{16,12},{20,16},{24,20},{28,24},{1,29},{... | collective-permute-start | bytes 1179656 | tf_op jit(solution)/shard_map/ppermute | solution.py:597
  114.4 0.0 collective-permute-done.24.refs_2_
  114.4 0.0 collective-permute-start.25
  114.4 0.0 copy-done.9
  114.4 0.0 copy-done.11
  114.4 0.0 copy-done.15
  114.5 0.0 copy-done.17
  114.5 0.0 copy-done.13
  114.5 11.3 %contract.8.refs_0_ = f32[768,256]{1,0:T(8,128)} custom-call(bf16[96,160,128]{2,1,0:T(8,128)(2,1)} %bitcast.9.amp_ref, s32[80,128]{1,0:T(8,128)S(1)} %get-tuple-element.406, bf16[12,128,128]{2,1,0:T(8,128)(2,1)} %copy-done.2, bf16[13,128,128]{2,1,0:T(8,128)(2,1)} %copy-done, bf16[12,128,128]{2,1,0:T(8,128)(2,1)} %copy-done.17, ...), custom_call_target="tpu_custom_call" | custom-call | flops 4026531840 | bytes 6000000 | tf_op jit(solution)/shard_map/contract/pallas_call | solution.py:380
  125.8 0.0 collective-permute-done.17.refs_3_
  125.8 0.0 collective-permute-done.20.refs_6_
  125.8 2.7 %collective-permute-start.28 = (bf16[13,128,128]{2,1,0:T(8,128)(2,1)S(1)}, bf16[13,128,128]{2,1,0:T(8,128)(2,1)S(1)}, u32[]{:S(2)}, u32[]{:S(2)}) collective-permute-start(bf16[13,128,128]{2,1,0:T(8,128)(2,1)S(1)} %collective-permute-done.20.refs_6_), channel_id=1, source_target_pairs={{0,28},{4,0},{8,4},{12,8},{16,12},{20,16},{24,20},{28,24},{1,29},{... | collective-permute-start | bytes 1277960 | tf_op jit(solution)/shard_map/ppermute | solution.py:612
  128.5 0.0 collective-permute-start.27
  128.6 0.0 collective-permute-done.26.refs_5_
  128.6 3.7 %collective-permute-done.25.refs_4_ = bf16[13,128,128]{2,1,0:T(8,128)(2,1)S(1)} collective-permute-done((bf16[13,128,128]{2,1,0:T(8,128)(2,1)S(1)}, bf16[13,128,128]{2,1,0:T(8,128)(2,1)S(1)}, u32[]{:S(2)}, u32[]{:S(2)}) %collective-permute-start.25) | collective-permute-done | bytes 426016 | tf_op jit(solution)/shard_map/ppermute | solution.py:597
  132.2 1.1 copy-done.4
  133.3 7.0 %contract.9 = (f32[768,256]{1,0:T(8,128)S(1)}, bf16[20,96,128]{2,1,0:T(8,128)(2,1)S(1)}) custom-call(bf16[96,160,128]{2,1,0:T(8,128)(2,1)} %bitcast.9.amp_ref, s32[80,128]{1,0:T(8,128)S(1)} %get-tuple-element.405, f32[768,256]{1,0:T(8,128)S(1)} %copy-done.4, bf16[12,128,128]{2,1,0:T(8,128)(2,1)S(1)} %collective-permute-done.16.refs_1_, ...), custom_call_target="tpu_custom_call" | custom-call | flops 4026531840 | bytes 6000000 | tf_op jit(solution)/shard_map/contract/pallas_call | solution.py:380
  140.4 0.0 collective-permute-done.27.low_hbm
  140.4 0.0 collective-permute-done.28.high_hbm
  140.4 3.2 %contract_last.4 = (f32[512,128]{1,0:T(8,128)S(1)}, f32[512,128]{1,0:T(8,128)S(1)}) custom-call(s32[1]{0:T(128)} %bitcast.6.core_ref, bf16[20,96,128]{2,1,0:T(8,128)(2,1)S(1)} %get-tuple-element.182.rest_hbm, s32[80,128]{1,0:T(8,128)S(1)} %get-tuple-element.405, f32[768,256]{1,0:T(8,128)S(1)} %get-tuple-element.183.start_hbm, ...), custom_call_target="tpu_custom_call" | custom-call | flops 1006632960 | bytes 3000000 | tf_op jit(solution)/shard_map/contract_last/pallas_call | solution.py:497
  143.6 2.2 %collective-permute-start.29 = (f32[512,128]{1,0:T(8,128)S(1)}, f32[512,128]{1,0:T(8,128)S(1)}, u32[]{:S(2)}, u32[]{:S(2)}) collective-permute-start(f32[512,128]{1,0:T(8,128)S(1)} %get-tuple-element.187), channel_id=1, source_target_pairs={{0,1},{1,0},{2,3},{3,2},{4,5},{5,4},{6,7},{7,6},{8,9},{9,8},{10,11... | collective-permute-start | bytes 786440 | tf_op jit(solution)/shard_map/ppermute | solution.py:617
  145.7 1.2 collective-permute-done.29
  146.9 10.6 %all_to_all.16.parts_ref = f32[16,32,128]{2,1,0:T(8,128)S(1)} all-to-all(f32[16,32,128]{2,1,0:T(8,128)S(1)} %bitcast.37), channel_id=1, replica_groups={{0,32,64,96,128,160,192,224,2,34,66,98,130,162,194,226},{1,33,65,97,129..., dimensions={0} | all-to-all | bytes 524288 | tf_op jit(solution)/shard_map/all_to_all | solution.py:619
  157.6 1.1 unpack.4
  (20 shorter events, 0.1 us)
Async XLA Ops:
  8.1 8.8 %copy-start.7 = (s32[800]{0:T(1024)S(1)}, s32[800]{0:T(1024)}, u32[]{:S(2)}) copy-start(s32[800]{0:T(1024)} %param.9) | copy-start | bytes 9604
  8.1 9.0 %copy-start.6 = (s32[1024]{0:T(1024)S(1)}, s32[1024]{0:T(1024)}, u32[]{:S(2)}) copy-start(s32[1024]{0:T(1024)} %param.10) | copy-start | bytes 12292
  8.1 61.0 %all-to-all-start.1 = ((bf16[32,3,160,128]{3,2,1,0:T(8,128)(2,1)}), bf16[32,3,160,128]{3,2,1,0:T(8,128)(2,1)}, u32[]{:S(2)}, u32[]{:S(2)}) async-start(bf16[32,3,160,128]{3,2,1,0:T(8,128)(2,1)} %bitcast.34), calls=%async_computation.1 | async-start | bytes 7864320 | tf_op jit(solution)/shard_map/all_to_all | solution.py:627
  17.1 13.0 %copy-start.8 = (s32[8]{0:T(128)S(1)}, s32[8]{0:T(128)}, u32[]{:S(2)}) copy-start(s32[8]{0:T(128)} %constant.97.clone) | copy-start | bytes 100
  24.3 45.5 %copy-start = (bf16[13,128,128]{2,1,0:T(8,128)(2,1)}, bf16[13,128,128]{2,1,0:T(8,128)(2,1)S(1)}, u32[]{:S(2)}) copy-start(bf16[13,128,128]{2,1,0:T(8,128)(2,1)S(1)} %get-tuple-element.177.refs_1_) | copy-start | bytes 1277956
  24.4 48.9 %copy-start.2 = (bf16[12,128,128]{2,1,0:T(8,128)(2,1)}, bf16[12,128,128]{2,1,0:T(8,128)(2,1)S(1)}, u32[]{:S(2)}) copy-start(bf16[12,128,128]{2,1,0:T(8,128)(2,1)S(1)} %get-tuple-element.176.refs_0_) | copy-start | bytes 1179652
  24.4 51.4 %collective-permute-start.18 = (bf16[13,128,128]{2,1,0:T(8,128)(2,1)S(1)}, bf16[13,128,128]{2,1,0:T(8,128)(2,1)S(1)}, u32[]{:S(2)}, u32[]{:S(2)}) collective-permute-start(bf16[13,128,128]{2,1,0:T(8,128)(2,1)S(1)} %get-tuple-element.177.refs_1_), channel_id=1, source_target_pairs={{0,28},{4,0},{8,4},{12,8},{16,12},{20,16},{24,20},{28,24},{1,29},{... | collective-permute-start | bytes 1277960 | tf_op jit(solution)/shard_map/ppermute | solution.py:597
  69.9 15.9 %collective-permute-start.22 = (bf16[13,128,128]{2,1,0:T(8,128)(2,1)S(1)}, bf16[13,128,128]{2,1,0:T(8,128)(2,1)S(1)}, u32[]{:S(2)}, u32[]{:S(2)}) collective-permute-start(bf16[13,128,128]{2,1,0:T(8,128)(2,1)S(1)} %get-tuple-element.177.refs_1_), channel_id=1, source_target_pairs={{0,4},{4,8},{8,12},{12,16},{16,20},{20,24},{24,28},{28,0},{1,5},{5... | collective-permute-start | bytes 1277960 | tf_op jit(solution)/shard_map/ppermute | solution.py:597
  71.6 22.6 %collective-permute-start.15 = (bf16[12,128,128]{2,1,0:T(8,128)(2,1)S(1)}, bf16[12,128,128]{2,1,0:T(8,128)(2,1)S(1)}, u32[]{:S(2)}, u32[]{:S(2)}) collective-permute-start(bf16[12,128,128]{2,1,0:T(8,128)(2,1)S(1)} %get-tuple-element.176.refs_0_), channel_id=1, source_target_pairs={{0,4},{4,8},{8,12},{12,16},{16,20},{20,24},{24,28},{28,0},{1,5},{5... | collective-permute-start | bytes 1179656 | tf_op jit(solution)/shard_map/ppermute | solution.py:597
  73.2 21.0 %collective-permute-start.21 = (bf16[12,128,128]{2,1,0:T(8,128)(2,1)S(1)}, bf16[12,128,128]{2,1,0:T(8,128)(2,1)S(1)}, u32[]{:S(2)}, u32[]{:S(2)}) collective-permute-start(bf16[12,128,128]{2,1,0:T(8,128)(2,1)S(1)} %get-tuple-element.176.refs_0_), channel_id=1, source_target_pairs={{0,28},{4,0},{8,4},{12,8},{16,12},{20,16},{24,20},{28,24},{1,29},{... | collective-permute-start | bytes 1179656 | tf_op jit(solution)/shard_map/ppermute | solution.py:597
  75.7 38.7 %copy-start.9 = (bf16[13,128,128]{2,1,0:T(8,128)(2,1)}, bf16[13,128,128]{2,1,0:T(8,128)(2,1)S(1)}, u32[]{:S(2)}) copy-start(bf16[13,128,128]{2,1,0:T(8,128)(2,1)S(1)} %collective-permute-done.18.refs_3_) | copy-start | bytes 1277956
  75.7 21.1 %collective-permute-start.19 = (bf16[13,128,128]{2,1,0:T(8,128)(2,1)S(1)}, bf16[13,128,128]{2,1,0:T(8,128)(2,1)S(1)}, u32[]{:S(2)}, u32[]{:S(2)}) collective-permute-start(bf16[13,128,128]{2,1,0:T(8,128)(2,1)S(1)} %collective-permute-done.18.refs_3_), channel_id=1, source_target_pairs={{0,28},{4,0},{8,4},{12,8},{16,12},{20,16},{24,20},{28,24},{1,29},{... | collective-permute-start | bytes 1277960 | tf_op jit(solution)/shard_map/ppermute | solution.py:597
  85.8 28.7 %copy-start.11 = (bf16[13,128,128]{2,1,0:T(8,128)(2,1)}, bf16[13,128,128]{2,1,0:T(8,128)(2,1)S(1)}, u32[]{:S(2)}) copy-start(bf16[13,128,128]{2,1,0:T(8,128)(2,1)S(1)} %collective-permute-done.22.refs_5_) | copy-start | bytes 1277956
  85.8 28.7 %collective-permute-start.24 = (bf16[13,128,128]{2,1,0:T(8,128)(2,1)S(1)}, bf16[13,128,128]{2,1,0:T(8,128)(2,1)S(1)}, u32[]{:S(2)}, u32[]{:S(2)}) collective-permute-start(bf16[13,128,128]{2,1,0:T(8,128)(2,1)S(1)} %collective-permute-done.22.refs_5_), channel_id=1, source_target_pairs={{0,4},{4,8},{8,12},{12,16},{16,20},{20,24},{24,28},{28,0},{1,5},{5... | collective-permute-start | bytes 1277960 | tf_op jit(solution)/shard_map/ppermute | solution.py:597
  94.2 20.3 %copy-start.15 = (bf16[12,128,128]{2,1,0:T(8,128)(2,1)}, bf16[12,128,128]{2,1,0:T(8,128)(2,1)S(1)}, u32[]{:S(2)}) copy-start(bf16[12,128,128]{2,1,0:T(8,128)(2,1)S(1)} %collective-permute-done.15.refs_4_) | copy-start | bytes 1179652
  94.2 17.6 %collective-permute-start.16 = (bf16[12,128,128]{2,1,0:T(8,128)(2,1)S(1)}, bf16[12,128,128]{2,1,0:T(8,128)(2,1)S(1)}, u32[]{:S(2)}, u32[]{:S(2)}) collective-permute-start(bf16[12,128,128]{2,1,0:T(8,128)(2,1)S(1)} %collective-permute-done.15.refs_4_), channel_id=1, source_target_pairs={{0,4},{4,8},{8,12},{12,16},{16,20},{20,24},{24,28},{28,0},{1,5},{5... | collective-permute-start | bytes 1179656 | tf_op jit(solution)/shard_map/ppermute | solution.py:597
  94.2 20.3 %copy-start.17 = (bf16[12,128,128]{2,1,0:T(8,128)(2,1)}, bf16[12,128,128]{2,1,0:T(8,128)(2,1)S(1)}, u32[]{:S(2)}) copy-start(bf16[12,128,128]{2,1,0:T(8,128)(2,1)S(1)} %collective-permute-done.21.refs_2_) | copy-start | bytes 1179652
  94.2 17.5 %collective-permute-start.23 = (bf16[12,128,128]{2,1,0:T(8,128)(2,1)S(1)}, bf16[12,128,128]{2,1,0:T(8,128)(2,1)S(1)}, u32[]{:S(2)}, u32[]{:S(2)}) collective-permute-start(bf16[12,128,128]{2,1,0:T(8,128)(2,1)S(1)} %collective-permute-done.21.refs_2_), channel_id=1, source_target_pairs={{0,28},{4,0},{8,4},{12,8},{16,12},{20,16},{24,20},{28,24},{1,29},{... | collective-permute-start | bytes 1179656 | tf_op jit(solution)/shard_map/ppermute | solution.py:597
  96.9 17.6 %copy-start.13 = (bf16[13,128,128]{2,1,0:T(8,128)(2,1)}, bf16[13,128,128]{2,1,0:T(8,128)(2,1)S(1)}, u32[]{:S(2)}) copy-start(bf16[13,128,128]{2,1,0:T(8,128)(2,1)S(1)} %collective-permute-done.19.refs_7_) | copy-start | bytes 1277956
  96.9 28.9 %collective-permute-start.20 = (bf16[13,128,128]{2,1,0:T(8,128)(2,1)S(1)}, bf16[13,128,128]{2,1,0:T(8,128)(2,1)S(1)}, u32[]{:S(2)}, u32[]{:S(2)}) collective-permute-start(bf16[13,128,128]{2,1,0:T(8,128)(2,1)S(1)} %collective-permute-done.19.refs_7_), channel_id=1, source_target_pairs={{0,28},{4,0},{8,4},{12,8},{16,12},{20,16},{24,20},{28,24},{1,29},{... | collective-permute-start | bytes 1277960 | tf_op jit(solution)/shard_map/ppermute | solution.py:597
  111.7 14.1 %collective-permute-start.17 = (bf16[12,128,128]{2,1,0:T(8,128)(2,1)S(1)}, bf16[12,128,128]{2,1,0:T(8,128)(2,1)S(1)}, u32[]{:S(2)}, u32[]{:S(2)}) collective-permute-start(bf16[12,128,128]{2,1,0:T(8,128)(2,1)S(1)} %collective-permute-done.16.refs_1_), channel_id=1, source_target_pairs={{0,4},{4,8},{8,12},{12,16},{16,20},{20,24},{24,28},{28,0},{1,5},{5... | collective-permute-start | bytes 1179656 | tf_op jit(solution)/shard_map/ppermute | solution.py:597
  111.7 2.7 %copy-start.19 = (bf16[12,128,128]{2,1,0:T(8,128)(2,1)}, bf16[12,128,128]{2,1,0:T(8,128)(2,1)S(1)}, u32[]{:S(2)}) copy-start(bf16[12,128,128]{2,1,0:T(8,128)(2,1)S(1)} %collective-permute-done.23.refs_6_) | copy-start | bytes 1179652
  111.7 16.8 %collective-permute-start.26 = (bf16[12,128,128]{2,1,0:T(8,128)(2,1)S(1)}, bf16[12,128,128]{2,1,0:T(8,128)(2,1)S(1)}, u32[]{:S(2)}, u32[]{:S(2)}) collective-permute-start(bf16[12,128,128]{2,1,0:T(8,128)(2,1)S(1)} %collective-permute-done.23.refs_6_), channel_id=1, source_target_pairs={{0,28},{4,0},{8,4},{12,8},{16,12},{20,16},{24,20},{28,24},{1,29},{... | collective-permute-start | bytes 1179656 | tf_op jit(solution)/shard_map/ppermute | solution.py:597
  114.4 17.8 %collective-permute-start.25 = (bf16[13,128,128]{2,1,0:T(8,128)(2,1)S(1)}, bf16[13,128,128]{2,1,0:T(8,128)(2,1)S(1)}, u32[]{:S(2)}, u32[]{:S(2)}) collective-permute-start(bf16[13,128,128]{2,1,0:T(8,128)(2,1)S(1)} %collective-permute-done.24.refs_2_), channel_id=1, source_target_pairs={{0,4},{4,8},{8,12},{12,16},{16,20},{20,24},{24,28},{28,0},{1,5},{5... | collective-permute-start | bytes 1277960 | tf_op jit(solution)/shard_map/ppermute | solution.py:597
  125.8 14.6 %collective-permute-start.28 = (bf16[13,128,128]{2,1,0:T(8,128)(2,1)S(1)}, bf16[13,128,128]{2,1,0:T(8,128)(2,1)S(1)}, u32[]{:S(2)}, u32[]{:S(2)}) collective-permute-start(bf16[13,128,128]{2,1,0:T(8,128)(2,1)S(1)} %collective-permute-done.20.refs_6_), channel_id=1, source_target_pairs={{0,28},{4,0},{8,4},{12,8},{16,12},{20,16},{24,20},{28,24},{1,29},{... | collective-permute-start | bytes 1277960 | tf_op jit(solution)/shard_map/ppermute | solution.py:612
  128.5 11.8 %collective-permute-start.27 = (bf16[12,128,128]{2,1,0:T(8,128)(2,1)S(1)}, bf16[12,128,128]{2,1,0:T(8,128)(2,1)S(1)}, u32[]{:S(2)}, u32[]{:S(2)}) collective-permute-start(bf16[12,128,128]{2,1,0:T(8,128)(2,1)S(1)} %collective-permute-done.17.refs_3_), channel_id=1, source_target_pairs={{0,4},{4,8},{8,12},{12,16},{16,20},{20,24},{24,28},{28,0},{1,5},{5... | collective-permute-start | bytes 1179656 | tf_op jit(solution)/shard_map/ppermute | solution.py:612
  132.2 1.1 copy-start.4
  143.6 3.3 %collective-permute-start.29 = (f32[512,128]{1,0:T(8,128)S(1)}, f32[512,128]{1,0:T(8,128)S(1)}, u32[]{:S(2)}, u32[]{:S(2)}) collective-permute-start(f32[512,128]{1,0:T(8,128)S(1)} %get-tuple-element.187), channel_id=1, source_target_pairs={{0,1},{1,0},{2,3},{3,2},{4,5},{5,4},{6,7},{7,6},{8,9},{9,8},{10,11... | collective-permute-start | bytes 786440 | tf_op jit(solution)/shard_map/ppermute | solution.py:617
